TPU v7x, 512 devices: a whole 4x4x16 slice. The times are simulated.
512 devices in a mesh: wide: 64 (over z, x_hi, core), narrow: 8 (over y, x_lo).
Axes of the slice: x: 4 (x_hi: 2, x_lo: 2; x = x_hi * 2 + x_lo), y: 4, z: 16, core: 2. Of those that a mesh axis runs over, the one named last changes fastest.
Arguments:
- panels: bfloat16 [64, 8192, 128], P('wide', 'narrow'), may hold values from -6 to 6
- stiff_blocks: bfloat16 [64, 1216, 4096], P('wide', 'narrow'), may hold values from -0.375 to 0.375
- mass_blocks: bfloat16 [64, 1216, 4096], P('wide', 'narrow'), may hold values from -0.375 to 0.375
- block_rows: int32 [64, 1216], P('wide', 'narrow'), may hold values from 0 to 16, as said below
- block_cols: int32 [64, 1216], P('wide', 'narrow'), may hold values from 0 to 127
- interface_map: int32 [64, 8192], P('wide', 'narrow'), may hold values from 0 to 8191, as said below
- cond_vectors: bfloat16 [8192, 768], P('narrow'), may hold values from -0.1875 to 0.1875
Outputs:
- condensed: bfloat16 [64, 8, 768, 512], P('wide', 'narrow')
Inputs may be any that keep to these rules, and one draw needn't show every extreme that they name: `block_rows`: in each partition's 152 slots the used slots come first; on some partition all 152 are used. `interface_map`: for every cell a permutation of the rows; of the 1024 rows of one partition at most 256 land in any one interface group, and in every cell some partition sends exactly 256 to some group.
All inputs are finite; a program needn't handle non-finite values.
Results may differ from a plain program's by a relative error of at most 0.0049.
Values may be sent and summed in bfloat16 or wider, within the bound.
A program may use at most 128 MiB of HBM per device.

v0:
```python
import jax
import jax.numpy as jnp
from jax import lax
from jax.sharding import PartitionSpec as P

BLK = 64
PC = 128
NC = 768
RB_DEV = 16
ROWS_DEV = 1024


def from_root(value, axis, source):
    kept = jnp.where(lax.axis_index(axis) == source, value, 0).astype(value.dtype)
    return lax.psum(kept, axis)


def body(panels, stiff_blocks, mass_blocks, block_rows, block_cols, interface_map, cond_vectors):
    group_count = lax.axis_size("narrow")
    cell_count = lax.axis_size("wide")
    slot_count = block_rows.shape[1]
    cell_blocks = RB_DEV * group_count
    peer_cap = 2 * ROWS_DEV // group_count
    stiffness = stiff_blocks.reshape(slot_count, BLK, BLK)
    mass_matrix = mass_blocks.reshape(slot_count, BLK, BLK)
    row_index = block_rows.reshape(slot_count)
    column_index = block_cols.reshape(slot_count)
    selector = (row_index[None, :] == jnp.arange(RB_DEV)[:, None]).astype(jnp.float32)
    owners = (0, cell_count // 2)
    panel_list = []
    for owner_index in owners:
        owner_rows = from_root(panels, "wide", owner_index)
        panel_list.append(lax.all_gather(owner_rows, "narrow", axis=1, tiled=True))
    pieces = []
    for panel_whole in panel_list:
        blocks = panel_whole.reshape(cell_blocks, BLK, PC)[column_index]
        for matrix in (stiffness, mass_matrix):
            product = jnp.einsum("sij,sjc->sic", matrix, blocks, preferred_element_type=jnp.float32)
            summed = jnp.einsum("rs,sic->ric", selector, product, precision=lax.Precision.HIGHEST)
            pieces.append(summed.reshape(ROWS_DEV, PC))
    product_rows = jnp.concatenate(pieces, axis=1).astype(jnp.bfloat16)
    position = interface_map.reshape(ROWS_DEV)
    target = position // ROWS_DEV
    slot_index = position % ROWS_DEV
    target_hits = (target[:, None] == jnp.arange(group_count)[None, :]).astype(jnp.int32)
    bucket_rank = jnp.sum(jnp.cumsum(target_hits, axis=0) * target_hits, axis=1) - 1
    send_rows = (
        jnp.zeros((group_count, peer_cap, 4 * PC), jnp.bfloat16)
        .at[target, bucket_rank]
        .set(product_rows)
    )
    send_slots = (
        jnp.full((group_count, peer_cap), ROWS_DEV, jnp.int32)
        .at[target, bucket_rank]
        .set(slot_index)
    )
    arrived, arrived_slots = (
        lax.all_to_all(send_rows, "narrow", split_axis=0, concat_axis=0, tiled=True),
        lax.all_to_all(send_slots, "narrow", split_axis=0, concat_axis=0, tiled=True),
    )
    placed = (
        jnp.zeros((ROWS_DEV, 4 * PC), jnp.bfloat16)
        .at[arrived_slots.reshape(-1)]
        .set(arrived.reshape(-1, 4 * PC), mode="drop")
    )
    condensed = lax.dot_general(
        cond_vectors, placed, (((0,), (0,)), ((), ())), preferred_element_type=jnp.float32
    )
    return condensed.astype(jnp.bfloat16).reshape(1, 1, NC, 4 * PC)


def solution(mesh):
    return jax.shard_map(
        body,
        mesh=mesh,
        in_specs=(
            P("wide", "narrow", None),
            P("wide", "narrow", None),
            P("wide", "narrow", None),
            P("wide", "narrow"),
            P("wide", "narrow"),
            P("wide", "narrow"),
            P("narrow", None),
        ),
        out_specs=P("wide", "narrow", None, None),
        check_vma=False,
    )
```

profile of v0, /device:TPU:1, one launch (start us, length us, event | category | flops | bytes accessed | tf_op | source)
XLA Modules:
  0.0 748.8 jit_solution(6269135097737931937)
XLA Ops:
  6.5 0.0 copy-start
  6.5 0.0 copy-start.5
  6.5 0.0 all-reduce.3.cloned.1.call-start
  6.5 1.9 broadcast_select_fusion.1
  8.5 0.0 all-reduce.3.cloned.1.call-update
  8.5 0.0 all-gather.3.cloned.1.call-start
  8.5 532.3 %all-reduce.3.cloned.1.call-done = (bf16[1,1024,128]{2,1,0:T(8,128)(2,1)}, bf16[1,1024,128]{2,1,0:T(8,128)(2,1)}) async-done(((bf16[1,1024,128]{2,1,0:T(8,128)(2,1)}, bf16[1,1024,128]{2,1,0:T(8,128)(2,1)}), (bf16[1,1024,128]{2,1,0:T(8,128)(2,1)}, bf16[1,1024,128]{2,1,0:T(8,128)(2,1)})) %all-reduce.3.cloned.1.call-update) | async-done | bytes 524304 | tf_op jit(solution)/shard_map/psum | solution.py:15
  540.8 0.0 all-gather.3.cloned.1.call-update
  540.9 0.0 all-gather.5.cloned.1.call-start
  540.9 0.7 all-gather.5.cloned.1.call-update
  541.6 0.7 add_select_fusion.1
  542.3 2.3 reduce-window.6
  544.6 0.3 slice_reduce_fusion
  544.8 0.2 reduce-window.9
  545.0 0.7 add_select_fusion
  545.7 0.1 add_bitcast_fusion
  545.8 0.7 compare_select_fusion.1
  546.5 0.7 multiply_reduce_fusion
  547.3 0.8 and_reduce_fusion
  548.0 4.9 scatter_custom_fusion.1
  552.9 4.0 all-to-all-start
  556.9 0.0 copy-done.5
  557.0 4.1 reshape.241
  561.0 0.0 copy-start.7
  561.0 4.8 reshape.243
  565.8 0.0 copy-done.7
  565.8 35.7 %all-gather.3.cloned.1.call-done = bf16[1,8192,128]{2,1,0:T(8,128)(2,1)} async-done(((bf16[1,1024,128]{2,1,0:T(8,128)(2,1)}), bf16[1,8192,128]{2,1,0:T(8,128)(2,1)}) %all-gather.3.cloned.1.call-update) | async-done | bytes 2097168 | tf_op jit(solution)/shard_map/all_gather | solution.py:33
  601.5 4.1 gather_fusion
  605.6 0.0 copy-start.1
  605.6 0.0 copy-start.4
  605.6 5.6 fusion.54
  611.2 0.0 copy-done.1
  611.2 0.0 copy-done.4
  611.2 3.0 fusion.55
  614.3 48.6 %all-gather.5.cloned.1.call-done = bf16[1,8192,128]{2,1,0:T(8,128)(2,1)} async-done(((bf16[1,1024,128]{2,1,0:T(8,128)(2,1)}), bf16[1,8192,128]{2,1,0:T(8,128)(2,1)}) %all-gather.5.cloned.1.call-update) | async-done | bytes 2097168 | tf_op jit(solution)/shard_map/all_gather | solution.py:33
  662.9 4.0 gather_fusion.1
  666.9 0.0 copy-start.2
  666.9 0.0 copy-start.3
  667.0 0.0 slice-start.2
  667.0 3.4 fusion.56
  670.4 0.0 copy-done.2
  670.4 0.5 copy-done.3
  670.9 0.8 fusion.57
  671.7 0.4 slice-done.2
  672.1 1.6 slice-done.3
  673.8 0.0 copy-done.6
  673.8 4.5 fusion.13
  678.3 0.0 slice-done
  678.3 0.0 slice-done.1
  678.3 4.7 fusion.16
  683.1 4.5 fusion.19
  687.6 4.5 fusion.22
  692.1 0.1 copy.9
  692.2 0.1 copy.10
  692.3 0.1 copy.11
  692.3 0.1 copy.12
  692.4 7.0 scatter_custom_fusion.2
  699.4 0.0 all-to-all-done
  699.4 4.3 all-to-all-start.1
  703.8 26.1 %all-to-all-done.1 = bf16[8,256,512]{2,1,0:T(8,128)(2,1)} async-done(((bf16[8,256,512]{2,1,0:T(8,128)(2,1)}), bf16[8,256,512]{2,1,0:T(8,128)(2,1)}, u32[]{:S(2)}, u32[]{:S(2)}) %all-to-all-start.1) | async-done | bytes 2097184 | tf_op jit(solution)/shard_map/all_to_all | solution.py:58
  729.9 10.2 %scatter_custom_fusion = bf16[1024,512]{1,0:T(8,128)(2,1)S(1)} fusion(s32[2048]{0:T(1024)S(1)} %bitcast.105, bf16[2048,512]{1,0:T(8,128)(2,1)} %bitcast.24, bf16[]{:T(256)} %constant.46.clone.1), kind=kCustom, calls=%fused_computation.32 | custom fusion | bytes 1049088 | tf_op jit(solution)/shard_map/scatter | solution.py:64
  740.1 0.0 copy-done
  740.1 1.0 fusion.12
  741.1 1.2 copy.13
  (13 shorter events, 0.1 us)
Async XLA Ops:
  6.5 733.6 %copy-start = (bf16[1024,768]{1,0:T(8,128)(2,1)S(1)}, bf16[1024,768]{1,0:T(8,128)(2,1)}, u32[]{:S(2)}) copy-start(bf16[1024,768]{1,0:T(8,128)(2,1)} %param.13) | copy-start | bytes 4718596
  6.5 550.4 %copy-start.5 = (bf16[1,152,4096]{2,1,0:T(8,128)(2,1)S(1)}, bf16[1,152,4096]{2,1,0:T(8,128)(2,1)}, u32[]{:S(2)}) copy-start(bf16[1,152,4096]{2,1,0:T(8,128)(2,1)} %param.8) | copy-start | bytes 3735556
  6.5 534.3 %all-reduce.3.cloned.1.call-start = ((), (), s32[]{:S(2)}) async-start(), calls=%async_computation.4 | async-start | bytes 1048576 | tf_op jit(solution)/shard_map/psum | solution.py:15
  8.5 593.0 %all-gather.3.cloned.1.call-start = ((), (), s32[]{:S(2)}) async-start(), calls=%async_computation.2 | async-start | bytes 2359296 | tf_op jit(solution)/shard_map/all_gather | solution.py:33
  540.9 122.0 %all-gather.5.cloned.1.call-start = ((), (), s32[]{:S(2)}) async-start(), calls=%async_computation.3 | async-start | bytes 2359296 | tf_op jit(solution)/shard_map/all_gather | solution.py:33
  552.9 146.5 %all-to-all-start = ((s32[8,1,256]{2,1,0:T(1,128)}), s32[8,1,256]{2,1,0:T(1,128)S(1)}, u32[]{:S(2)}, u32[]{:S(2)}) async-start(s32[8,1,256]{2,1,0:T(1,128)} %bitcast.6), calls=%async_computation | async-start | bytes 16384 | tf_op jit(solution)/shard_map/all_to_all | solution.py:59
  561.0 4.8 copy-start.7
  605.6 5.6 copy-start.1
  605.6 5.6 copy-start.4
  666.9 3.4 copy-start.2
  666.9 3.9 copy-start.3
  667.0 5.2 slice-start.2
  667.0 11.3 %slice-start = ((s8[4980736]{0:T(1024)(128)(4,1)}), s8[4194304]{0:T(1024)(128)(4,1)S(1)}, s32[]{:S(2)}) async-start(s8[4980736]{0:T(1024)(128)(4,1)} %bitcast.84), calls=%async_computation.5 | async-start | bytes 8388608
  670.9 2.9 slice-start.3
  670.9 2.9 copy-start.6
  670.9 7.4 slice-start.1
  699.4 30.5 %all-to-all-start.1 = ((bf16[8,256,512]{2,1,0:T(8,128)(2,1)}), bf16[8,256,512]{2,1,0:T(8,128)(2,1)}, u32[]{:S(2)}, u32[]{:S(2)}) async-start(bf16[8,256,512]{2,1,0:T(8,128)(2,1)} %bitcast.88), calls=%async_computation.1 | async-start | bytes 4194304 | tf_op jit(solution)/shard_map/all_to_all | solution.py:58
Sparse Core Ops, SparseCore 0:
  10.3 530.4 all-reduce.2
  543.1 58.3 all-gather.2
  603.8 59.0 all-gather.4
where the time goes:
time: 749 us
  waiting for transfers between devices  643 us (86%)
  local copies, waits for them, and re-layouts  36.4 us (5%)
  matrix products  32.2 us (4%)
  other arithmetic  15.1 us (2%)
  between operations  13.3 us (2%)
  starting transfers between devices  8.44 us (1%)
    psum x1, waiting for transfers between devices, from_root(): return lax.psum(kept, axis)  532 us
    all_gather x2, waiting for transfers between devices, body(): panel_list.append(lax.all_gather(owner_rows, 'narrow', axis=1, tiled=True))  84.3 us
    all_to_all x1, waiting for transfers between devices, body(): lax.all_to_all(send_rows, 'narrow', split_axis=0, concat_axis=0, tiled=True)  26.1 us
    dot_general x4, matrix products, body(): jnp.einsum('rs,sic->ric', selector, product, precision=lax.Precision.HIGH...  18.3 us
  transfers between devices with their start and end apart: 5, of which 4 were waited for; matrix products, arithmetic and copies ran while one was open for 9% of the time, Pallas kernels for 0%

commit v1 on v0

--- a/solution.py
+++ b/solution.py
@@ -12,7 +12,7 @@
 
 def from_root(value, axis, source):
     kept = jnp.where(lax.axis_index(axis) == source, value, 0).astype(value.dtype)
-    return lax.psum(kept, axis)
+    return jnp.sum(lax.all_gather(kept, axis), axis=0)
 
 
 def body(panels, stiff_blocks, mass_blocks, block_rows, block_cols, interface_map, cond_vectors):

time: 749 us -> 614 us (0.82)
  waiting for transfers between devices: 643 us -> 495 us
  other arithmetic: 15.1 us -> 30.6 us
    psum x1 -> x0, waiting for transfers between devices: 532 us -> none  [from_root(): return lax.psum(kept, axis)]
    all_gather x0 -> x2, waiting for transfers between devices: none -> 385 us  [from_root(): return jnp.sum(lax.all_gather(kept, axis), axis=0)]
    reduce_sum x0 -> x2, other arithmetic: none -> 19 us  [from_root(): return jnp.sum(lax.all_gather(kept, axis), axis=0)]
  transfers between devices with their start and end apart: 5 -> 6, of which waited for: 4 -> 5; matrix products, arithmetic and copies ran while one was open for 9% -> 12% of each run, Pallas kernels for 0% -> 0%
where the time goes in v1:
time: 614 us; the launch traced here: 609 us
  waiting for transfers between devices  495 us (81%)
  local copies, waits for them, and re-layouts  36.7 us (6%)
  other arithmetic  30.6 us (5%)
  matrix products  25.1 us (4%)
  between operations  13.6 us (2%)
  starting transfers between devices  8.51 us (1%)
    all_gather x2, waiting for transfers between devices, from_root(): return jnp.sum(lax.all_gather(kept, axis), axis=0)  385 us
    all_gather x2, waiting for transfers between devices, body(): panel_list.append(lax.all_gather(owner_rows, 'narrow', axis=1, tiled=True))  82.5 us
    all_to_all x1, waiting for transfers between devices, body(): lax.all_to_all(send_rows, 'narrow', split_axis=0, concat_axis=0, tiled=True)  26.1 us
    reduce_sum x2, other arithmetic, from_root(): return jnp.sum(lax.all_gather(kept, axis), axis=0)  19 us
    dot_general x4, matrix products, body(): jnp.einsum('rs,sic->ric', selector, product, precision=lax.Precision.HIGH...  18.3 us
  transfers between devices with their start and end apart: 6, of which 5 were waited for; matrix products, arithmetic and copies ran while one was open for 12% of the time, Pallas kernels for 0%

profile of v1, /device:TPU:1, one launch (start us, length us, event | category | flops | bytes accessed | tf_op | source)
XLA Modules:
  0.0 609.3 jit_solution(3030305789585106457)
XLA Ops:
  6.5 0.0 copy-start
  6.5 0.0 all-gather.13.cloned.1.call-start
  6.5 1.9 broadcast_select_fusion.1
  8.4 0.0 all-gather.13.cloned.1.call-update
  8.5 0.0 all-gather.9.cloned.1.call-start
  8.5 0.7 all-gather.9.cloned.1.call-update
  9.2 0.0 all-gather.15.cloned.1.call-start
  9.3 202.1 %all-gather.13.cloned.1.call-done = bf16[64,1024,128]{2,1,0:T(8,128)(2,1)} async-done(((bf16[1,1024,128]{2,1,0:T(8,128)(2,1)}), bf16[64,1024,128]{2,1,0:T(8,128)(2,1)}) %all-gather.13.cloned.1.call-update) | async-done | bytes 16777232 | tf_op jit(solution)/shard_map/all_gather | solution.py:15
  211.4 9.5 %reduce.9 = bf16[1024,128]{1,0:T(8,128)(2,1)} reduce(bf16[64,1024,128]{2,1,0:T(8,128)(2,1)} %all-gather.13.cloned.1.call-done, bf16[]{:T(256)} %constant.49.clone.1), dimensions={0}, to_apply=%region_5.6 | reduce | flops 8257536 | bytes 17039362 | tf_op jit(solution)/shard_map/reduce_sum | solution.py:15
  220.9 0.0 all-gather.15.cloned.1.call-update
  220.9 0.0 copy-start.6
  220.9 0.0 copy-start.10
  220.9 0.0 copy-start.9
  220.9 0.0 copy-start.5
  220.9 0.0 all-gather.11.cloned.1.call-start
  221.0 183.3 %all-gather.9.cloned.1.call-done = bf16[64,1024,128]{2,1,0:T(8,128)(2,1)} async-done(((bf16[1,1024,128]{2,1,0:T(8,128)(2,1)}), bf16[64,1024,128]{2,1,0:T(8,128)(2,1)}) %all-gather.9.cloned.1.call-update) | async-done | bytes 16777232 | tf_op jit(solution)/shard_map/all_gather | solution.py:15
  404.3 9.5 %reduce.8 = bf16[1024,128]{1,0:T(8,128)(2,1)} reduce(bf16[64,1024,128]{2,1,0:T(8,128)(2,1)} %all-gather.9.cloned.1.call-done, bf16[]{:T(256)} %constant.49.clone.1), dimensions={0}, to_apply=%region_4.5 | reduce | flops 8257536 | bytes 17039362 | tf_op jit(solution)/shard_map/reduce_sum | solution.py:15
  413.8 0.0 all-gather.11.cloned.1.call-update
  413.8 0.0 copy-done.6
  413.8 2.3 reduce-window.6
  416.1 0.3 slice_reduce_fusion
  416.4 0.2 reduce-window.9
  416.6 0.1 add_bitcast_fusion
  416.7 0.0 copy-done.10
  416.7 0.1 multiply_reduce_fusion
  416.8 0.0 copy-done.9
  416.8 0.1 and_reduce_fusion
  416.9 4.9 scatter_custom_fusion.1
  421.8 4.0 all-to-all-start
  425.8 0.0 copy-done.5
  425.8 4.1 reshape.243
  429.9 0.0 copy-start.8
  429.9 5.2 reshape.245
  435.1 0.0 copy-done.8
  435.1 25.5 %all-gather.15.cloned.1.call-done = bf16[8192,128]{1,0:T(8,128)(2,1)} async-done(((bf16[1024,128]{1,0:T(8,128)(2,1)}), bf16[8192,128]{1,0:T(8,128)(2,1)}) %all-gather.15.cloned.1.call-update) | async-done | bytes 2097168 | tf_op jit(solution)/shard_map/all_gather | solution.py:33
  460.6 4.1 gather_fusion.1
  464.7 57.0 %all-gather.11.cloned.1.call-done = bf16[8192,128]{1,0:T(8,128)(2,1)} async-done(((bf16[1024,128]{1,0:T(8,128)(2,1)}), bf16[8192,128]{1,0:T(8,128)(2,1)}) %all-gather.11.cloned.1.call-update) | async-done | bytes 2097168 | tf_op jit(solution)/shard_map/all_gather | solution.py:33
  521.7 4.1 gather_fusion
  525.9 0.0 copy-start.2
  525.9 3.4 convolution_bitcast_fusion.2
  529.3 0.0 copy-done.2
  529.3 0.5 copy-done.4
  529.8 0.8 convolution_bitcast_fusion.3
  530.6 0.9 copy-done.3
  531.5 0.8 convolution_bitcast_fusion.1
  532.3 0.9 copy-done.1
  533.2 0.8 convolution_bitcast_fusion
  534.0 0.0 copy-done.7
  534.0 4.5 fusion.12
  538.6 4.7 fusion.9
  543.3 4.5 fusion.15
  547.8 4.5 fusion.18
  552.3 0.1 copy.17
  552.4 0.1 copy.15
  552.5 0.1 copy.19
  552.5 0.1 copy.21
  552.6 7.0 %scatter_custom_fusion.2 = bf16[2048,512]{1,0:T(8,128)(2,1)} fusion(s32[1024]{0:T(1024)S(1)} %broadcast_select_fusion.2, bf16[1024,128]{1,0:T(8,128)(2,1)S(1)} %bitcast.81, bf16[]{:T(256)} %constant.84, bf16[1024,128]{1,0:T(8,128)(2,1)S(1)} %bitcast.80, bf16[1024,128]{1,0:T(8,128)(2,1)S(1)} %bitcast.78, bf16[1024,128]{1,0:T(8,128)(2,1)S(1)} %bitcast.79, ...), kind=kCustom, calls=%fused_computation.23 | custom fusion | flops 4194304 | bytes 3145732
  559.6 0.0 all-to-all-done
  559.6 4.4 all-to-all-start.1
  564.0 26.1 %all-to-all-done.1 = bf16[8,256,512]{2,1,0:T(8,128)(2,1)} async-done(((bf16[8,256,512]{2,1,0:T(8,128)(2,1)}), bf16[8,256,512]{2,1,0:T(8,128)(2,1)}, u32[]{:S(2)}, u32[]{:S(2)}) %all-to-all-start.1) | async-done | bytes 2097184 | tf_op jit(solution)/shard_map/all_to_all | solution.py:58
  590.1 10.2 %scatter_custom_fusion = bf16[1024,512]{1,0:T(8,128)(2,1)S(1)} fusion(s32[2048]{0:T(1024)S(1)} %bitcast.92, bf16[2048,512]{1,0:T(8,128)(2,1)} %bitcast.24, bf16[]{:T(256)} %constant.49.clone.1), kind=kCustom, calls=%fused_computation.32 | custom fusion | bytes 1049088 | tf_op jit(solution)/shard_map/scatter | solution.py:64
  600.3 0.0 copy-done
  600.3 1.0 fusion.8
  601.4 1.2 copy.22
  (14 shorter events, 0.1 us)
Async XLA Ops:
  6.5 593.8 %copy-start = (bf16[1024,768]{1,0:T(8,128)(2,1)S(1)}, bf16[1024,768]{1,0:T(8,128)(2,1)}, u32[]{:S(2)}) copy-start(bf16[1024,768]{1,0:T(8,128)(2,1)} %param.13) | copy-start | bytes 4718596
  6.5 204.9 %all-gather.13.cloned.1.call-start = ((), (), s32[]{:S(2)}) async-start(), calls=%async_computation.4 | async-start | bytes 17039360 | tf_op jit(solution)/shard_map/all_gather | solution.py:15
  8.5 395.8 %all-gather.9.cloned.1.call-start = ((), (), s32[]{:S(2)}) async-start(), calls=%async_computation.2 | async-start | bytes 17039360 | tf_op jit(solution)/shard_map/all_gather | solution.py:15
  9.2 451.4 %all-gather.15.cloned.1.call-start = ((), (), s32[]{:S(2)}) async-start(), calls=%async_computation.5 | async-start | bytes 2359296 | tf_op jit(solution)/shard_map/all_gather | solution.py:33
  220.9 192.9 %copy-start.6 = (s32[1,1024]{1,0:T(1,128)S(1)}, s32[1,1024]{1,0:T(1,128)}, u32[]{:S(2)}) copy-start(s32[1,1024]{1,0:T(1,128)} %param.12) | copy-start | bytes 12292
  220.9 195.8 %copy-start.10 = (s32[2]{0:T(128)S(1)}, s32[2]{0:T(128)}, u32[]{:S(2)}) copy-start(s32[2]{0:T(128)} %constant.68) | copy-start | bytes 28
  220.9 195.9 %copy-start.9 = (s32[2]{0:T(128)S(1)}, s32[2]{0:T(128)}, u32[]{:S(2)}) copy-start(s32[2]{0:T(128)} %constant.71) | copy-start | bytes 28
  220.9 204.9 %copy-start.5 = (bf16[1,152,4096]{2,1,0:T(8,128)(2,1)S(1)}, bf16[1,152,4096]{2,1,0:T(8,128)(2,1)}, u32[]{:S(2)}) copy-start(bf16[1,152,4096]{2,1,0:T(8,128)(2,1)} %param.8) | copy-start | bytes 3735556
  220.9 300.8 %all-gather.11.cloned.1.call-start = ((), (), s32[]{:S(2)}) async-start(), calls=%async_computation.3 | async-start | bytes 2359296 | tf_op jit(solution)/shard_map/all_gather | solution.py:33
  421.8 137.8 %all-to-all-start = ((s32[8,1,256]{2,1,0:T(1,128)}), s32[8,1,256]{2,1,0:T(1,128)S(1)}, u32[]{:S(2)}, u32[]{:S(2)}) async-start(s32[8,1,256]{2,1,0:T(1,128)} %bitcast.6), calls=%async_computation | async-start | bytes 16384 | tf_op jit(solution)/shard_map/all_to_all | solution.py:59
  429.9 5.2 copy-start.8
  525.9 3.4 copy-start.2
  525.9 3.9 copy-start.4
  529.8 1.7 copy-start.3
  531.5 1.7 copy-start.1
  533.2 0.8 copy-start.7
  559.6 30.5 %all-to-all-start.1 = ((bf16[8,256,512]{2,1,0:T(8,128)(2,1)}), bf16[8,256,512]{2,1,0:T(8,128)(2,1)}, u32[]{:S(2)}, u32[]{:S(2)}) async-start(bf16[8,256,512]{2,1,0:T(8,128)(2,1)} %bitcast.75), calls=%async_computation.1 | async-start | bytes 4194304 | tf_op jit(solution)/shard_map/all_to_all | solution.py:58
Sparse Core Ops, SparseCore 0:
  10.6 200.7 all-gather.12
  214.7 189.5 all-gather.8
  406.4 54.2 all-gather.14
  462.6 59.1 all-gather.10
